TPU v7x, 128 devices: a whole 4x4x4 slice. The times are simulated.
128 devices in a mesh: grp: 4 (over y), sub: 32 (over x, z, core).
Axes of the slice: x: 4, y: 4, z: 4, core: 2. Of those that a mesh axis runs over, the one named last changes fastest.
Arguments:
- modes: bfloat16 [48, 64, 512, 256], P(None, 'grp', 'sub'), as said below
- counts: int32 [128], P(('grp', 'sub')), may hold values from 8 to 40, as said below
- kappa: bfloat16 [64, 512, 256], P('grp', 'sub'), may hold values from 0.29882812 to 3
- react: bfloat16 [64, 512, 256], P('grp', 'sub'), may hold values from 0.19921875 to 2
Outputs:
- factored: float32 [6144, 6144], P(('grp', 'sub'))
Inputs may be any that keep to these rules, and one draw needn't show every extreme that they name: A subdomain's live slots are its first counts of 48; at least one subdomain has 40 and one has 8. `modes`: entries of slots at or beyond a subdomain's count are not used.
All inputs are finite; a program needn't handle non-finite values.
Results may differ from a plain program's by a relative error of at most 0.00065.
Values may be sent and summed in bfloat16 or wider, within the bound.
A program may use at most 256 MiB of HBM per device.

v0:
```python
import jax
import jax.numpy as jnp
from jax import lax
from jax.experimental import pallas as pl
from jax.experimental.pallas import tpu as pltpu
from jax.sharding import PartitionSpec as P

F32 = jnp.float32
BF16 = jnp.bfloat16
MESH = pl.DeviceIdType.MESH
NG, NU = 4, 32
CX, CY, NZ = 16, 16, 256
SLOTS, LIVE = 48, 40
NB = 22
DONE = 1024
GROUP = 24
NC = SLOTS * NG * NU


def nt(a, b, precision=None):
    return lax.dot_general(
        a, b, (((1,), (1,)), ((), ())), preferred_element_type=F32, precision=precision
    )


def lanes_of(shape):
    return lax.broadcasted_iota(jnp.int32, shape, len(shape) - 1)


def rows_of(shape):
    return lax.broadcasted_iota(jnp.int32, shape, len(shape) - 2)


def split(x):
    hi = x.astype(BF16)
    return hi, (x - hi.astype(F32)).astype(BF16)


def pad_rows(x, rows):
    return jnp.concatenate([x, jnp.zeros((rows - x.shape[0], x.shape[1]), x.dtype)], 0)


def pad_lanes(x, lanes):
    return jnp.concatenate([x, jnp.zeros((x.shape[0], lanes - x.shape[1]), x.dtype)], 1)


def transposed(x):
    return jnp.transpose(pad_rows(x, 128))


def assemble_kernel(
    count_ref, modes_ref, kappa_ref, react_ref, blocks_ref, links_ref, pivots_ref,
    raw, kappa, react, field, masked, wx, wy, wz, diag, edge, halo, face_x, face_y,
    high, low, ends, links, pivs, order,
    raw_sem, cell_sem, halo_send, halo_recv, face_send, face_recv,
    up_sem, link_send, link_recv, piv_send, piv_recv, cross_send, cross_recv,
):
    g, u = lax.axis_index("grp"), lax.axis_index("sub")
    partners = [
        (lax.rem(g + NG - 1, NG), u),
        (lax.rem(g + 1, NG), u),
        (g, lax.rem(u + NU - 1, NU)),
        (g, lax.rem(u + 1, NU)),
    ]
    inside = [g > 0, g < NG - 1, u > 0, u < NU - 1]
    mirror = [1, 0, 3, 2]
    chip, core = u // 2, lax.rem(u, 2)
    joined = (g < 2) & (u < GROUP)

    def fetch(x):
        return pltpu.make_async_copy(
            modes_ref.at[pl.ds(0, LIVE), x], raw.at[x], raw_sem.at[x]
        )

    cells = [
        pltpu.make_async_copy(kappa_ref, kappa, cell_sem.at[0]),
        pltpu.make_async_copy(react_ref, react, cell_sem.at[1]),
    ]
    cells[0].start()
    for x in [0, CX - 1] + list(range(1, CX - 1)):
        fetch(x).start()
    cells[1].start()

    barrier = pltpu.get_barrier_semaphore()

    def greet(device):
        pl.semaphore_signal(barrier, inc=1, device_id=device, device_id_type=MESH)

    for partner in partners:
        greet(partner)

    def others(count, me, act):
        for step in range(1, count):
            v = me + step
            act(jnp.where(v >= count, v - count, v))

    @pl.when(joined)
    def _():
        others(GROUP // 2, chip, lambda v: greet((g, 2 * v + core)))
        greet((g, 2 * chip + 1 - core))

    count = count_ref[0]
    z_from, z_to = rows_of((NZ, NZ)), lanes_of((NZ, NZ))
    here = z_from == jnp.where(z_to < 128, 2 * z_to, 2 * z_to - 255)
    order[...] = jnp.where(here, 1.0, 0.0).astype(BF16)

    def ordered(x):
        return jnp.dot(x.reshape(-1, NZ), order[...], preferred_element_type=F32)

    cells[0].wait()
    kap = ordered(kappa[...]).reshape(CX, CY, NZ)
    edge[0] = kap[0]
    edge[1] = kap[CX - 1]
    for x in range(CX):
        edge[2, x : x + 1] = kap[x, 0:1]
        edge[3, x : x + 1] = kap[x, CY - 1 : CY]

    live = rows_of((CY, LIVE, NZ)) < count

    def turn(x, side=None):
        plane = jnp.swapaxes(ordered(raw[x]).reshape(LIVE, CY, NZ), 0, 1)
        plane = jnp.where(live, plane, 0.0)
        field[x] = plane
        for y in range(CY):
            masked[x, :, NZ * y : NZ * (y + 1)] = pad_rows(plane[y], SLOTS).astype(BF16)
        if side is not None:
            for y in range(0, CY, 2):
                two = jnp.concatenate([plane[y], plane[y + 1]], 0)
                ends[side, :, NZ * y // 2 : NZ * (y + 2) // 2] = two.astype(BF16)

    fetch(0).wait()
    fetch(CX - 1).wait()
    turn(0, 0)
    turn(CX - 1, 1)
    pl.semaphore_wait(barrier, jnp.where(joined, GROUP // 2 + 4, 4))

    def halo_copy(k):
        return pltpu.make_async_remote_copy(
            src_ref=edge.at[k], dst_ref=halo.at[mirror[k]],
            send_sem=halo_send.at[k], recv_sem=halo_recv.at[mirror[k]],
            device_id=partners[k], device_id_type=MESH,
        )

    sources = [
        ends.at[0],
        ends.at[1],
        masked.at[:, :, pl.ds(0, NZ)],
        masked.at[:, :, pl.ds((CY - 1) * NZ, NZ)],
    ]
    landings = [face_x.at[0], face_x.at[1], face_y.at[0], face_y.at[1]]

    def face_copy(k):
        return pltpu.make_async_remote_copy(
            src_ref=sources[k], dst_ref=landings[mirror[k]],
            send_sem=face_send.at[k], recv_sem=face_recv.at[mirror[k]],
            device_id=partners[k], device_id_type=MESH,
        )

    for k in range(4):
        halo_copy(k).start()
    face_copy(0).start()
    face_copy(1).start()

    def turn_next(i, carry):
        fetch(2 * i + 1).wait()
        fetch(2 * i + 2).wait()
        turn(2 * i + 1)
        turn(2 * i + 2)
        return carry

    lax.fori_loop(0, CX // 2 - 1, turn_next, 0)
    face_copy(2).start()
    face_copy(3).start()

    plane0 = jnp.zeros((CY, NZ), F32)
    row0 = jnp.zeros((1, NZ), F32)
    half = lanes_of((CY, 128))
    wx[0] = plane0
    wx[CX] = plane0
    for x in range(CX - 1):
        wx[x + 1] = 0.5 * (kap[x] + kap[x + 1])
    for x in range(CX):
        k = kap[x]
        wy[x, 0:1] = row0
        wy[x, 1:CY] = 0.5 * (k[: CY - 1] + k[1:])
        wy[x, CY : CY + 1] = row0
        even, uneven = k[:, :128], k[:, 128:]
        wz[x, :, 0:128] = 0.5 * (even + uneven)
        wz[x, :, 128:] = jnp.where(half == 127, 0.0, 0.5 * (uneven + pltpu.roll(even, 127, 1)))
    cells[1].wait()
    reac = ordered(react[...]).reshape(CX, CY, NZ)
    for k in range(4):
        halo_copy(k).wait_recv()
    ext = [jnp.where(inside[k], halo[k], 0.0) for k in range(4)]
    bound = [0.5 * (edge[k] + ext[k]) for k in range(4)]
    for x in range(CX):
        k = kap[x]
        inner, outer = wz[x, :, 0:128], wz[x, :, 128:]
        below = jnp.where(half == 0, 0.5 * k[:, :128], pltpu.roll(outer, 1, 1))
        above = jnp.where(half == 127, 0.5 * k[:, 128:], outer)
        dz = jnp.concatenate([below + inner, inner + above], 1)
        dx = (bound[0] if x == 0 else wx[x]) + (bound[1] if x == CX - 1 else wx[x + 1])
        dy = wy[x, 0:CY] + wy[x, 1 : CY + 1]
        dy = dy + jnp.concatenate(
            [bound[2][x : x + 1], jnp.zeros((CY - 2, NZ), F32), bound[3][x : x + 1]], 0
        )
        diag[x] = reac[x] + dx + dy + dz

    def apply(x, gram):
        before, after = jnp.maximum(x - 1, 0), jnp.minimum(x + 1, CX - 1)
        behind, v = None, field[x, 0]
        for y in range(CY):
            ahead = field[x, y + 1] if y < CY - 1 else None
            out = diag[x, y : y + 1] * v
            out = out - wx[x, y : y + 1] * field[before, y]
            out = out - wx[x + 1, y : y + 1] * field[after, y]
            if y > 0:
                out = out - wy[x, y : y + 1] * behind
            if y < CY - 1:
                out = out - wy[x, y + 1 : y + 2] * ahead
            even, uneven = v[:, :128], v[:, 128:]
            inner, outer = wz[x, y : y + 1, 0:128], wz[x, y : y + 1, 128:]
            out = out - jnp.concatenate(
                [
                    inner * uneven + pltpu.roll(outer * uneven, 1, 1),
                    inner * even + outer * pltpu.roll(even, 127, 1),
                ],
                1,
            )
            local = pad_rows(out, SLOTS).astype(BF16)
            gram = gram + nt(masked[x, :, NZ * y : NZ * (y + 1)], local)
            behind, v = v, ahead
        return gram

    gram = lax.fori_loop(
        0, CX // 2, lambda i, gram: apply(2 * i + 1, apply(2 * i, gram)),
        jnp.zeros((SLOTS, SLOTS), F32),
    )
    own = pad_lanes(gram, 128)
    spot, slot = lanes_of((SLOTS, 128)), rows_of((SLOTS, 128))
    own = own + jnp.where((spot == slot) & (slot >= count), 1.0, 0.0)
    sym = jnp.where(spot < LIVE, 0.5 * (own + transposed(own)[:SLOTS]), 0.0)

    on_diag = jnp.where((spot == slot) & (spot < LIVE), sym, 0.0)
    scale_lane = lax.rsqrt(jnp.sum(on_diag, axis=0, keepdims=True))
    scale_lane = jnp.where(lanes_of((1, 128)) < LIVE, scale_lane, 1.0)
    scale_row = lax.rsqrt(jnp.sum(on_diag, axis=1, keepdims=True)[:LIVE])

    def up_copy(ref, i):
        return pltpu.make_async_remote_copy(
            src_ref=ref, dst_ref=ref, send_sem=up_sem.at[i], recv_sem=up_sem.at[i + 2],
            device_id=(1, u), device_id_type=MESH,
        )

    def link_copy(to, owner):
        return pltpu.make_async_remote_copy(
            src_ref=links.at[owner, core], dst_ref=links.at[owner, core],
            send_sem=link_send.at[to], recv_sem=link_recv.at[owner],
            device_id=(g, 2 * to + core), device_id_type=MESH,
        )

    def piv_copy(to, owner):
        return pltpu.make_async_remote_copy(
            src_ref=pivs.at[owner, core], dst_ref=pivs.at[owner, core],
            send_sem=piv_send.at[to], recv_sem=piv_recv.at[owner],
            device_id=(g, 2 * to + core), device_id_type=MESH,
        )

    def cross_copy(ref, sem):
        return pltpu.make_async_remote_copy(
            src_ref=ref, dst_ref=ref, send_sem=cross_send.at[sem], recv_sem=cross_recv.at[sem],
            device_id=(g, 2 * chip + 1 - core), device_id_type=MESH,
        )

    def cross_link(v, c):
        return cross_copy(links.at[v, c], v)

    def cross_pivs(c):
        return cross_copy(pivs.at[:, c], GROUP // 2)

    link_up, piv_up = up_copy(links.at[chip, core], 0), up_copy(pivs.at[chip, core], 1)

    @pl.when(joined & (g == 0))
    def _():
        unit = sym[:LIVE] * scale_row * scale_lane
        packed = unit[0:16] + pltpu.roll(unit[16:32], LIVE, 1)
        packed = packed + pltpu.roll(pad_rows(unit[32:40], 16), 2 * LIVE, 1)
        shifted = pltpu.roll(jnp.broadcast_to(scale_lane, (16, 128)), 2 * LIVE, 1)
        wide_lane = lanes_of((16, 128))
        spare = (rows_of((16, 128)) == 8) & (wide_lane >= 2 * LIVE) & (wide_lane < 3 * LIVE)
        pivs[chip, core] = jnp.where(spare, shifted, packed)
        piv_up.start()
        others(GROUP // 2, chip, lambda v: piv_copy(v, chip).start())

    def coupling(k):
        weight = bound[k]
        total = jnp.zeros((SLOTS, SLOTS), F32)
        if k < 2:
            x = 0 if k == 0 else CX - 1
            for y in range(0, CY, 2):
                two = [field[x, j] * weight[j : j + 1] for j in (y, y + 1)]
                hi, lo = split(jnp.concatenate(two, 0))
                cols = slice(NZ * y // 2, NZ * (y + 2) // 2)
                high[:, cols], low[:, cols] = hi, lo
            face_copy(mirror[k]).wait_recv()
            both = nt(high[...], face_x[k]) + nt(low[...], face_x[k])
            both = pad_lanes(both, 128)
            block = both[:LIVE] + pltpu.roll(both[LIVE:], 128 - LIVE, 1)
            block = jnp.where(lanes_of((LIVE, 128)) < LIVE, block, 0.0)
        else:
            face_copy(mirror[k]).wait_recv()
            for x in range(CX):
                mine = field[x, 0 if k == 2 else CY - 1] * weight[x : x + 1]
                hi, lo = split(pad_rows(mine, SLOTS))
                other = face_y[k - 2, x]
                total = total + (nt(hi, other) + nt(lo, other))
            block = pad_lanes(total, 128)[:LIVE]
        return jnp.where(inside[k], -block, 0.0)

    found = {k: coupling(k) for k in (1, 3)}
    lane = lanes_of((LIVE, 128))
    odd = core == 1
    ahead = found[3] * scale_row
    ahead_t = transposed(found[3])[:LIVE] * scale_lane
    rising = transposed(found[1])[:LIVE] * scale_lane
    message = jnp.where(odd, ahead, ahead_t) + pltpu.roll(jnp.where(odd, ahead_t, ahead), LIVE, 1)
    message = message + pltpu.roll(rising, 2 * LIVE, 1)
    message = jnp.where(lane >= 3 * LIVE, count.astype(F32), message)
    message = jnp.where(lane == 3 * LIVE + 1, scale_row, message)

    @pl.when(joined & (g == 0))
    def _():
        links[chip, core] = message
        link_up.start()
        others(GROUP // 2, chip, lambda v: link_copy(v, chip).start())

    @pl.when(joined & (g == 1))
    def _():
        piv_up.wait_recv()
        others(GROUP // 2, chip, lambda v: piv_copy(v, chip).start())
        link_up.wait_recv()
        others(GROUP // 2, chip, lambda v: link_copy(v, chip).start())

    for k in (0, 2):
        found[k] = coupling(k)
    blocks_ref[0] = own
    for k in range(4):
        blocks_ref[k + 1] = pad_rows(found[k], SLOTS)
    blocks_ref[5] = sym

    @pl.when(joined)
    def _():
        others(GROUP // 2, chip, lambda v: piv_copy(chip, v).wait_recv())
        cross_pivs(core).start()
        cross_link(chip, core).start()

        def forward(v):
            link_copy(chip, v).wait_recv()
            cross_link(v, core).start()

        others(GROUP // 2, chip, forward)
        cross_pivs(1 - core).wait_recv()
        for v in range(GROUP // 2):
            cross_link(v, 1 - core).wait_recv()
        for v in range(GROUP):
            links_ref[v] = links[v // 2, v % 2]
            pivots_ref[v] = pivs[v // 2, v % 2]
        others(GROUP // 2, chip, lambda v: link_copy(v, chip).wait_send())
        others(GROUP // 2, chip, lambda v: piv_copy(v, chip).wait_send())
        cross_pivs(core).wait_send()
        for v in range(GROUP // 2):
            cross_link(v, core).wait_send()

    @pl.when(joined & (g == 0))
    def _():
        link_up.wait_send()
        piv_up.wait_send()

    for k in range(4):
        halo_copy(k).wait_send()
        face_copy(k).wait_send()


def assemble(count, modes, kappa, react):
    vmem = pl.BlockSpec(memory_space=pltpu.VMEM)
    hbm = pl.BlockSpec(memory_space=pltpu.HBM)
    dma = pltpu.SemaphoreType.DMA
    return pl.pallas_call(
        assemble_kernel,
        out_shape=(
            jax.ShapeDtypeStruct((6, SLOTS, 128), F32),
            jax.ShapeDtypeStruct((GROUP, LIVE, 128), F32),
            jax.ShapeDtypeStruct((GROUP, 16, 128), F32),
        ),
        in_specs=[pl.BlockSpec(memory_space=pltpu.SMEM), hbm, hbm, hbm],
        out_specs=(vmem, vmem, vmem),
        scratch_shapes=[
            pltpu.VMEM((CX, LIVE, CY, NZ), BF16),
            pltpu.VMEM((CX, CY, NZ), BF16),
            pltpu.VMEM((CX, CY, NZ), BF16),
            pltpu.VMEM((CX, CY, LIVE, NZ), F32),
            pltpu.VMEM((CX, SLOTS, CY * NZ), BF16),
            pltpu.VMEM((CX + 1, CY, NZ), F32),
            pltpu.VMEM((CX, 24, NZ), F32),
            pltpu.VMEM((CX, CY, NZ), F32),
            pltpu.VMEM((CX, CY, NZ), F32),
            pltpu.VMEM((4, 16, NZ), F32),
            pltpu.VMEM((4, 16, NZ), F32),
            pltpu.VMEM((2, 2 * LIVE, 8 * NZ), BF16),
            pltpu.VMEM((2, 16, SLOTS, NZ), BF16),
            pltpu.VMEM((2 * LIVE, 8 * NZ), BF16),
            pltpu.VMEM((2 * LIVE, 8 * NZ), BF16),
            pltpu.VMEM((2, 2 * LIVE, 8 * NZ), BF16),
            pltpu.VMEM((GROUP // 2, 2, LIVE, 128), F32),
            pltpu.VMEM((GROUP // 2, 2, 16, 128), F32),
            pltpu.VMEM((NZ, NZ), BF16),
            dma((CX,)),
            dma((2,)),
            dma((4,)),
            dma((4,)),
            dma((4,)),
            dma((4,)),
            dma((4,)),
            dma((GROUP // 2,)),
            dma((GROUP // 2,)),
            dma((GROUP // 2,)),
            dma((GROUP // 2,)),
            dma((GROUP // 2 + 1,)),
            dma((GROUP // 2 + 1,)),
        ],
        compiler_params=pltpu.CompilerParams(
            collective_id=0, has_side_effects=True, vmem_limit_bytes=50 * 2**20
        ),
        name="assemble",
    )(count, modes, kappa, react)


def halves(x, rows, axis):
    hi, lo = split(pad_rows(x, rows) if x.shape[0] < rows else x)
    return jnp.concatenate([hi, lo], axis)


def joined_halves(out, rows):
    tall = out.shape[0] // 2
    return out[:rows, :128] + (out[:rows, 128:] + out[tall : tall + rows, :128])


def nn3(a, b):
    left = halves(a, SLOTS, 0)
    out = jnp.dot(left, halves(b, 128, 1), preferred_element_type=F32)
    return joined_halves(out, a.shape[0])


def nt3(a, b):
    out = nt(halves(a, SLOTS, 0), halves(b, 128, 0))
    return joined_halves(out, a.shape[0])


def wide(x):
    return jnp.broadcast_to(x, (8, 128))


def pivots(p, soff, state, spread_ref, rows_ref, side_ref):
    tiles, saved = (list(part) for part in state)
    sub = rows_of((8, 128))
    at = soff + 8 * p
    column = lambda v, c: wide(tiles[v][:, c : c + 1])
    if p == 0:
        for c in range(8):
            spread_ref[p, c] = column(p, at + c)
    rows_ref[p] = tiles[p]
    d = {(i, j): wide(spread_ref[p, j, i : i + 1]) for i in range(8) for j in range(i, 8)}
    rows = [wide(rows_ref[p, c : c + 1]) for c in range(8)]
    follow = p + 1 < LIVE // 8
    if follow:
        under = [column(p + 1, at + c) for c in range(8)]
        coming = [column(p + 1, at + 8 + c) for c in range(8)]
    others = [v for v in range(LIVE // 8) if v not in (p, p + 1)]
    factors = {v: [column(v, at + c) for c in range(8)] for v in others}
    alpha, beta, z = {}, {}, list(rows)
    for c in range(0, 8, 2):
        n = c + 1
        a, b, e = d[c, c], d[c, n], d[n, n]
        det = a * e - b * b
        r = pl.reciprocal(det, approx=True)
        for i in range(n + 1, 8):
            top, bottom = e * d[c, i] - b * d[n, i], a * d[n, i] - b * d[c, i]
            alpha[c, i], beta[c, i] = top * r, bottom * r
            for j in range(i, 8):
                if j <= n + 2:
                    d[i, j] = d[i, j] - (top * d[c, j] + bottom * d[n, j]) * r
                else:
                    d[i, j] = d[i, j] - (alpha[c, i] * d[c, j] + beta[c, i] * d[n, j])
        root = lax.rsqrt(a)
        saved[p] = jnp.where(sub == c, rows[c] * root, saved[p])
        second = (rows[n] - (b * root * root) * rows[c]) * (lax.rsqrt(det) * (a * root))
        saved[p] = jnp.where(sub == n, second, saved[p])
        for i in range(n + 1, 8):
            rows[i] = rows[i] - (alpha[c, i] * rows[c] + beta[c, i] * rows[n])
        z[c] = (e * rows[c] - b * rows[n]) * r
        z[n] = (a * rows[n] - b * rows[c]) * r
        if follow:
            first = (e * under[c] - b * under[n]) * r
            other = (a * under[n] - b * under[c]) * r
            side_ref[p, c], side_ref[p, n] = first, other
            for i in range(n + 1, 8):
                under[i] = under[i] - (alpha[c, i] * under[c] + beta[c, i] * under[n])
            for i in range(8):
                coming[i] = coming[i] - (
                    under[c] * wide(side_ref[p, c, i : i + 1])
                    + under[n] * wide(side_ref[p, n, i : i + 1])
                )
            tiles[p + 1] = tiles[p + 1] - (first * rows[c] + other * rows[n])
    if follow:
        for c in range(8):
            spread_ref[p + 1, c] = coming[c]
    for c in range(4, -1, -2):
        for i in range(c + 2, 8):
            z[c] = z[c] - alpha[c, i] * z[i]
            z[c + 1] = z[c + 1] - beta[c, i] * z[i]
    for v in others:
        terms = [factors[v][c] * z[c] for c in range(8)]
        while len(terms) > 1:
            terms = [terms[i] + terms[i + 1] for i in range(0, len(terms), 2)]
        tiles[v] = tiles[v] - terms[0]
    for c in range(8):
        tiles[p] = jnp.where(sub == c, z[c], tiles[p])
    return tuple(tiles), tuple(saved)


def place(out_ref, block, pos, keep):
    base = jnp.minimum((pos // 128) * 128, NC - 256)
    base = pl.multiple_of(base, 128)
    shifted = pltpu.roll(pad_lanes(block, 256), pos - base, 1)
    cols = lanes_of((SLOTS, 256)) + base
    out_ref[:, pl.ds(base, 256)] += jnp.where(keep(cols), shifted, 0.0)


def factor_kernel(
    links_ref, pivots_ref, blocks_ref, out_ref, linv_ref, k_ref, g_ref, f_ref, x_ref, spread_ref, rows_ref, side_ref,
):
    g, u = lax.axis_index("grp"), lax.axis_index("sub")
    s = g * NU + u
    upper = s <= 21
    member = (s == 21) | (s == 22) | ((s >= NU) & (s < NU + NB))
    lane = lanes_of((LIVE, 128))
    row = rows_of((LIVE, 128))
    lane48 = lanes_of((SLOTS, 128))
    row48 = rows_of((SLOTS, 128))
    out_ref[...] = jnp.zeros_like(out_ref)
    before = lambda cols: cols < DONE
    after = lambda cols: cols >= DONE

    def left(x, by):
        x = pltpu.roll(x, 128 - by, 1) if by else x
        return jnp.where(lanes_of(x.shape) < LIVE, x, 0.0)

    def put(block, pos, late):
        base = pos // 128 * 128
        shifted = pltpu.roll(pad_lanes(block, 256), pos - base, 1) if pos > base else (
            pad_lanes(block, 256)
        )
        if base < DONE < base + 256:
            cols = lanes_of((SLOTS, 256)) + base
            shifted = jnp.where(cols >= DONE if late else cols < DONE, shifted, 0.0)
        out_ref[:, base : base + 256] += shifted

    def reduce_row(q):
        at, wide_enough = jnp.maximum(q, 0), jnp.where(q == NB - 1, 16, LIVE)
        mine = jnp.where(q == s, blocks_ref[5], 0.0)
        mine = jnp.where(q == s - 1, blocks_ref[3], mine)
        mine = jnp.where(q == s - NU, blocks_ref[1], mine)
        mine = mine * scale(at, 0)
        held = jnp.where(q > 0, f_ref[jnp.maximum(q - 1, 0)], 0.0)
        f = mine - nn3(held, pad_rows(k_ref[at], 128))
        f_ref[at] = jnp.where((q <= s) & (lane48 < wide_enough), f, 0.0)

    def solve_row(q):
        at = jnp.maximum(q, 0)
        x = nt3(f_ref[at], pad_rows(linv_ref[at], 128))
        x_ref[at] = jnp.where((q == s) & (lane48 > row48), 0.0, x)

    def double_row(q):
        at = jnp.maximum(q, 0)
        x = x_ref[at]
        g_ref[at] = nn3(x, pad_rows(linv_ref[at], 128))

    def pivot_block(t, at):
        packed = pivots_ref[t]
        parts = []
        for i in range(3):
            by = (at - LIVE * i) % 128
            parts.append(pltpu.roll(packed, by, 1) if by else packed)
        block = jnp.concatenate([parts[0], parts[1], parts[2][:8]], 0)
        return jnp.where((lane >= at) & (lane < at + LIVE), block, 0.0)

    def scale(t, at):
        spare = pltpu.roll(pivots_ref[t, 8:16, :], (at - 2 * LIVE) % 128, 1)[0:1]
        lanes = lanes_of((1, 128))
        return jnp.where((lanes >= at) & (lanes < at + LIVE), spare, 1.0)

    def live_count(t):
        return jnp.max(jnp.where(lanes_of((8, 128)) == 3 * LIVE, links_ref[t][0:8], 0.0))

    def at_rows(x, start):
        above = jnp.zeros((start, 128), F32)
        return pad_rows(jnp.concatenate([above, x], 0) if start else x, 128)

    def step(t, odd, scur, n):
        soff, uoff = (LIVE, 0) if odd else (0, LIVE)
        following = jnp.minimum(t + 1, NB - 1)
        given = links_ref[t] * scale(following, uoff)
        limit = jnp.where(t == NB - 1, 16, LIVE)
        in_s = (lane >= soff) & (lane < soff + LIVE)
        in_u = (lane >= uoff) & (lane < uoff + LIVE)
        eye = jnp.where(lane == row + soff, 1.0, 0.0)
        a = jnp.where((row < limit) & (lane < soff + limit), scur, eye)
        rest = jnp.where(lane == row + 2 * LIVE, 1.0, 0.0)
        rest = jnp.where(in_u, jnp.where(row < limit, given, 0.0), rest)
        a = jnp.where(in_s, a, rest)
        ut = jnp.where(in_s, given, 0.0) * links_ref[following, :, 3 * LIVE + 1 : 3 * LIVE + 2]
        tiles = tuple(a[8 * v : 8 * v + 8] for v in range(LIVE // 8))
        state = pivots(0, soff, (tiles, tiles), spread_ref, rows_ref, side_ref)

        double_row(t - 3)
        solve_row(t - 2)
        reduce_row(t - 1)
        coming, coming_n = pivot_block(following, uoff), live_count(following)
        n = jnp.where(t == NB - 1, jnp.minimum(n, 16.0), n)
        for p in range(1, LIVE // 8):
            state = lax.cond(
                n > 8.0 * p,
                lambda st, p=p: pivots(p, soff, st, spread_ref, rows_ref, side_ref),
                lambda st: st,
                state,
            )
        tiles, saved = state
        k = jnp.concatenate(tiles, 0)
        snext = coming - nn3(ut, at_rows(k, soff))
        linv_ref[t] = left(jnp.concatenate(saved, 0), 2 * LIVE)
        k_ref[t + 1] = left(k, uoff)
        return snext, coming_n

    @pl.when(upper | member)
    def _():
        k_ref[0] = jnp.zeros((LIVE, 128), F32)
        linv_ref[0] = jnp.zeros((LIVE, 128), F32)
        f_ref[0] = jnp.zeros((SLOTS, 128), F32)
        x_ref[0] = jnp.zeros((SLOTS, 128), F32)
        def pair(i, carry):
            carry = step(2 * i, False, *carry)
            return step(2 * i + 1, True, *carry)

        lax.fori_loop(0, NB // 2, pair, (pivot_block(0, 0), live_count(0)))
        double_row(NB - 3)
        solve_row(NB - 2)
        reduce_row(NB - 1)
        double_row(NB - 2)
        solve_row(NB - 1)
        double_row(NB - 1)
        for t in range(NB):
            put(x_ref[t], SLOTS * t, False)

    @pl.when(upper)
    def _():
        dead = jnp.where((row48 == lane48) & (row48 >= LIVE), 1.0, 0.0)
        place(out_ref, dead, SLOTS * s, before)

    @pl.when(member)
    def _():
        late = lane >= 16
        last = jnp.where(row < 16, links_ref[NB - 1], 0.0)
        own = jnp.where(late & (row < 16), pivot_block(NB - 1, 0) / scale(NB - 1, 0), 0.0)
        over = jnp.where(late, left(links_ref[NB - 2], LIVE), 0.0)
        y = None
        for t in range(NB - 1, -1, -1):
            if y is None:
                y = g_ref[t]
                put(-nn3(y, pad_rows(left(last, 0), 128)), SLOTS * NB, True)
                put(-nn3(y, pad_rows(own, 128)), SLOTS * (NB - 1), True)
            else:
                y = g_ref[t] - nt3(y, pad_rows(k_ref[t + 1], 128))
            if t == NB - 2:
                put(-nn3(y, pad_rows(over, 128)), SLOTS * (NB - 1), True)
            rising = pad_rows(left(links_ref[t], 2 * LIVE), 128)
            put(-nt3(y, rising), SLOTS * (t + NU), True)

    @pl.when(s >= 21)
    def _():
        targets = [s, s - NU, s + NU, s - 1, s + 1]
        valid = [True, g > 0, g < NG - 1, u > 0, u < NU - 1]
        for k in range(5):
            pos = SLOTS * jnp.clip(targets[k], 0, NG * NU - 1)
            place(out_ref, jnp.where(valid[k], blocks_ref[k], 0.0), pos, after)

    @pl.when(s == 21)
    def _():
        out_ref[0:16, DONE:] = jnp.zeros((16, NC - DONE), F32)


def factor(links, pivs, blocks):
    vmem = pl.BlockSpec(memory_space=pltpu.VMEM)
    return pl.pallas_call(
        factor_kernel,
        out_shape=jax.ShapeDtypeStruct((SLOTS, NC), F32),
        in_specs=[vmem, vmem, vmem],
        out_specs=vmem,
        scratch_shapes=[
            pltpu.VMEM((NB, LIVE, 128), F32),
            pltpu.VMEM((NB + 1, LIVE, 128), F32),
            pltpu.VMEM((NB, SLOTS, 128), F32),
            pltpu.VMEM((NB, SLOTS, 128), F32),
            pltpu.VMEM((NB, SLOTS, 128), F32),
            pltpu.VMEM((LIVE // 8, 8, 8, 128), F32),
            pltpu.VMEM((LIVE // 8, 8, 128), F32),
            pltpu.VMEM((LIVE // 8, 8, 8, 128), F32),
        ],
        compiler_params=pltpu.CompilerParams(vmem_limit_bytes=40 * 2**20),
        name="factor",
    )(links, pivs, blocks)


def per_device(modes, counts, kappa, react):
    kappa = pltpu.with_memory_space_constraint(kappa, pltpu.HBM)
    react = pltpu.with_memory_space_constraint(react, pltpu.HBM)
    blocks, links, pivs = assemble(counts, modes, kappa, react)
    return factor(links, pivs, blocks)


def solution(mesh):
    in_specs = (
        P(None, "grp", "sub", None),
        P(("grp", "sub")),
        P("grp", "sub", None),
        P("grp", "sub", None),
    )
    out_specs = P(("grp", "sub"), None)
    return jax.shard_map(
        per_device, mesh=mesh, in_specs=in_specs, out_specs=out_specs, check_vma=False
    )
```

profile of v0, /device:TPU:9, one launch (start us, length us, event | category | flops | bytes accessed | tf_op | source)
XLA Modules:
  0.0 51.5 jit_solution(3397793742502743365)
XLA Ops:
  0.7 29.4 %assemble.1 = (f32[6,48,128]{2,1,0:T(8,128)S(1)}, f32[24,40,128]{2,1,0:T(8,128)S(1)}, f32[24,16,128]{2,1,0:T(8,128)S(1)}) custom-call(s32[1]{0:T(128)S(6)} %copy.5.count_ref, bf16[48,16,16,256]{3,2,1,0:T(8,128)(2,1)} %modes_ref.1, bf16[16,16,256]{2,1,0:T(8,128)(2,1)} %kappa_ref.1, bf16[16,16,256]{2,1,0:T(8,128)(2,1)} %react_ref.1), custom_call_target="tpu_custom_call" | custom-call | tf_op jit(solution)/shard_map/assemble/pallas_call | solution.py:388
  30.0 21.5 %factor.1 = f32[48,6144]{1,0:T(8,128)} custom-call(f32[24,40,128]{2,1,0:T(8,128)S(1)} %get-tuple-element.8.links_ref, f32[24,16,128]{2,1,0:T(8,128)S(1)} %get-tuple-element.9.pivots_ref, f32[6,48,128]{2,1,0:T(8,128)S(1)} %get-tuple-element.10.blocks_ref), custom_call_target="tpu_custom_call" | custom-call | tf_op jit(solution)/shard_map/factor/pallas_call | solution.py:703
where the time goes:
time: 51.7 us; the launch traced here: 51.5 us
  Pallas kernels  50.9 us (98%)
  between operations  0.66 us (1%)
    pallas_call x1, Pallas kernels, assemble(): pl.pallas_call(assemble_kernel, out_shape=(jax.ShapeDtypeStruct((6, SLOTS...  29.4 us
    pallas_call x1, Pallas kernels, factor(): pl.pallas_call(factor_kernel, out_shape=jax.ShapeDtypeStruct((SLOTS, NC),...  21.5 us

commit v1 on v0

--- a/solution.py
+++ b/solution.py
@@ -51,8 +51,8 @@
 def assemble_kernel(
     count_ref, modes_ref, kappa_ref, react_ref, blocks_ref, links_ref, pivots_ref,
     raw, kappa, react, field, masked, wx, wy, wz, diag, edge, halo, face_x, face_y,
-    high, low, ends, links, pivs, order,
-    raw_sem, cell_sem, halo_send, halo_recv, face_send, face_recv,
+    high, low, ends, links, pivs, order, upward, part, part_in,
+    raw_sem, cell_sem, halo_send, halo_recv, face_send, face_recv, piece_send, piece_recv, part_send, part_recv,
     up_sem, link_send, link_recv, piv_send, piv_recv, cross_send, cross_recv,
 ):
     g, u = lax.axis_index("grp"), lax.axis_index("sub")
@@ -117,21 +117,27 @@
 
     live = rows_of((CY, LIVE, NZ)) < count
 
-    def turn(x, side=None):
+    def turn(x):
         plane = jnp.swapaxes(ordered(raw[x]).reshape(LIVE, CY, NZ), 0, 1)
         plane = jnp.where(live, plane, 0.0)
         field[x] = plane
         for y in range(CY):
             masked[x, :, NZ * y : NZ * (y + 1)] = pad_rows(plane[y], SLOTS).astype(BF16)
-        if side is not None:
-            for y in range(0, CY, 2):
-                two = jnp.concatenate([plane[y], plane[y + 1]], 0)
-                ends[side, :, NZ * y // 2 : NZ * (y + 2) // 2] = two.astype(BF16)
-
-    fetch(0).wait()
-    fetch(CX - 1).wait()
-    turn(0, 0)
-    turn(CX - 1, 1)
+        return plane
+
+    def turn_two(x, w, q):
+        fetch(x).wait()
+        fetch(w).wait()
+        one, two = turn(x), turn(w)
+        for side, y in ((2, 0), (3, CY - 1)):
+            pair = jnp.concatenate([one[y], two[y]], 0).astype(BF16)
+            ends[side, :, pl.ds(pl.multiple_of(q * NZ, NZ), NZ)] = pair
+        return one, two
+
+    for side, plane in enumerate(turn_two(0, CX - 1, 0)):
+        for y in range(0, CY, 2):
+            pair = jnp.concatenate([plane[y], plane[y + 1]], 0).astype(BF16)
+            ends[side, :, NZ * y // 2 : NZ * (y + 2) // 2] = pair
     pl.semaphore_wait(barrier, jnp.where(joined, GROUP // 2 + 4, 4))
 
     def halo_copy(k):
@@ -141,18 +147,18 @@
             device_id=partners[k], device_id_type=MESH,
         )
 
-    sources = [
-        ends.at[0],
-        ends.at[1],
-        masked.at[:, :, pl.ds(0, NZ)],
-        masked.at[:, :, pl.ds((CY - 1) * NZ, NZ)],
-    ]
-    landings = [face_x.at[0], face_x.at[1], face_y.at[0], face_y.at[1]]
-
     def face_copy(k):
         return pltpu.make_async_remote_copy(
-            src_ref=sources[k], dst_ref=landings[mirror[k]],
+            src_ref=ends.at[k, :, pl.ds(4 * NZ * k, 4 * NZ)], dst_ref=face_x.at[mirror[k]],
             send_sem=face_send.at[k], recv_sem=face_recv.at[mirror[k]],
+            device_id=partners[k], device_id_type=MESH,
+        )
+
+    def piece_copy(k, q):
+        cols = pl.ds(pl.multiple_of(q * NZ, NZ), NZ)
+        return pltpu.make_async_remote_copy(
+            src_ref=ends.at[k, :, cols], dst_ref=face_y.at[mirror[k] - 2, :, cols],
+            send_sem=piece_send.at[k - 2, q], recv_sem=piece_recv.at[mirror[k] - 2, q],
             device_id=partners[k], device_id_type=MESH,
         )
 
@@ -160,21 +166,20 @@
         halo_copy(k).start()
     face_copy(0).start()
     face_copy(1).start()
+    piece_copy(2, 0).start()
+    piece_copy(3, 0).start()
 
     def turn_next(i, carry):
-        fetch(2 * i + 1).wait()
-        fetch(2 * i + 2).wait()
-        turn(2 * i + 1)
-        turn(2 * i + 2)
+        turn_two(2 * i + 1, 2 * i + 2, i + 1)
+        piece_copy(2, i + 1).start()
+        piece_copy(3, i + 1).start()
         return carry
 
     lax.fori_loop(0, CX // 2 - 1, turn_next, 0)
-    face_copy(2).start()
-    face_copy(3).start()
 
     plane0 = jnp.zeros((CY, NZ), F32)
     row0 = jnp.zeros((1, NZ), F32)
-    half = lanes_of((CY, 128))
+    lane128 = lanes_of((CY, 128))
     wx[0] = plane0
     wx[CX] = plane0
     for x in range(CX - 1):
@@ -186,7 +191,7 @@
         wy[x, CY : CY + 1] = row0
         even, uneven = k[:, :128], k[:, 128:]
         wz[x, :, 0:128] = 0.5 * (even + uneven)
-        wz[x, :, 128:] = jnp.where(half == 127, 0.0, 0.5 * (uneven + pltpu.roll(even, 127, 1)))
+        wz[x, :, 128:] = jnp.where(lane128 == 127, 0.0, 0.5 * (uneven + pltpu.roll(even, 127, 1)))
     cells[1].wait()
     reac = ordered(react[...]).reshape(CX, CY, NZ)
     for k in range(4):
@@ -196,8 +201,8 @@
     for x in range(CX):
         k = kap[x]
         inner, outer = wz[x, :, 0:128], wz[x, :, 128:]
-        below = jnp.where(half == 0, 0.5 * k[:, :128], pltpu.roll(outer, 1, 1))
-        above = jnp.where(half == 127, 0.5 * k[:, 128:], outer)
+        below = jnp.where(lane128 == 0, 0.5 * k[:, :128], pltpu.roll(outer, 1, 1))
+        above = jnp.where(lane128 == 127, 0.5 * k[:, 128:], outer)
         dz = jnp.concatenate([below + inner, inner + above], 1)
         dx = (bound[0] if x == 0 else wx[x]) + (bound[1] if x == CX - 1 else wx[x + 1])
         dy = wy[x, 0:CY] + wy[x, 1 : CY + 1]
@@ -246,9 +251,9 @@
     scale_lane = jnp.where(lanes_of((1, 128)) < LIVE, scale_lane, 1.0)
     scale_row = lax.rsqrt(jnp.sum(on_diag, axis=1, keepdims=True)[:LIVE])
 
-    def up_copy(ref, i):
+    def up_copy(src, dst, i):
         return pltpu.make_async_remote_copy(
-            src_ref=ref, dst_ref=ref, send_sem=up_sem.at[i], recv_sem=up_sem.at[i + 2],
+            src_ref=src, dst_ref=dst, send_sem=up_sem.at[i], recv_sem=up_sem.at[i + 2],
             device_id=(1, u), device_id_type=MESH,
         )
 
@@ -278,7 +283,15 @@
     def cross_pivs(c):
         return cross_copy(pivs.at[:, c], GROUP // 2)
 
-    link_up, piv_up = up_copy(links.at[chip, core], 0), up_copy(pivs.at[chip, core], 1)
+    def part_copy(k):
+        return pltpu.make_async_remote_copy(
+            src_ref=part.at[k], dst_ref=part_in.at[mirror[k]],
+            send_sem=part_send.at[k], recv_sem=part_recv.at[mirror[k]],
+            device_id=partners[k], device_id_type=MESH,
+        )
+
+    link_up = up_copy(upward, links.at[chip, core], 0)
+    piv_up = up_copy(pivs.at[chip, core], pivs.at[chip, core], 1)
 
     @pl.when(joined & (g == 0))
     def _():
@@ -292,57 +305,73 @@
         piv_up.start()
         others(GROUP // 2, chip, lambda v: piv_copy(v, chip).start())
 
+    x_order = [0, CX - 1] + list(range(1, CX - 1))
+
     def coupling(k):
-        weight = bound[k]
-        total = jnp.zeros((SLOTS, SLOTS), F32)
         if k < 2:
-            x = 0 if k == 0 else CX - 1
-            for y in range(0, CY, 2):
-                two = [field[x, j] * weight[j : j + 1] for j in (y, y + 1)]
-                hi, lo = split(jnp.concatenate(two, 0))
-                cols = slice(NZ * y // 2, NZ * (y + 2) // 2)
-                high[:, cols], low[:, cols] = hi, lo
+            cells = range(8) if k == 1 else range(8, CY)
+            mine = [field[0 if k == 0 else CX - 1, y] * bound[k][y : y + 1] for y in cells]
+        else:
+            mine = [field[x, 0 if k == 2 else CY - 1] * bound[k][x : x + 1] for x in x_order]
+        for q in range(len(mine) // 2):
+            hi, lo = split(jnp.concatenate(mine[2 * q : 2 * q + 2], 0))
+            cols = slice(NZ * q, NZ * (q + 1))
+            high[:, cols], low[:, cols] = hi, lo
+        width = NZ * len(mine) // 2
+        if k < 2:
             face_copy(mirror[k]).wait_recv()
-            both = nt(high[...], face_x[k]) + nt(low[...], face_x[k])
-            both = pad_lanes(both, 128)
-            block = both[:LIVE] + pltpu.roll(both[LIVE:], 128 - LIVE, 1)
-            block = jnp.where(lanes_of((LIVE, 128)) < LIVE, block, 0.0)
+            other = face_x[k]
         else:
-            face_copy(mirror[k]).wait_recv()
-            for x in range(CX):
-                mine = field[x, 0 if k == 2 else CY - 1] * weight[x : x + 1]
-                hi, lo = split(pad_rows(mine, SLOTS))
-                other = face_y[k - 2, x]
-                total = total + (nt(hi, other) + nt(lo, other))
-            block = pad_lanes(total, 128)[:LIVE]
+            for q in range(8):
+                piece_copy(mirror[k], q).wait_recv()
+            other = face_y[k - 2]
+        both = pad_lanes(nt(high[:, :width], other) + nt(low[:, :width], other), 128)
+        block = both[:LIVE] + pltpu.roll(both[LIVE:], 128 - LIVE, 1)
+        block = jnp.where(lanes_of((LIVE, 128)) < LIVE, block, 0.0)
         return jnp.where(inside[k], -block, 0.0)
 
-    found = {k: coupling(k) for k in (1, 3)}
+    half = {1: coupling(1), 0: coupling(0)}
+    for k in (1, 0):
+        part[k] = half[k]
+        part_copy(k).start()
+    found = {3: coupling(3)}
     lane = lanes_of((LIVE, 128))
     odd = core == 1
     ahead = found[3] * scale_row
     ahead_t = transposed(found[3])[:LIVE] * scale_lane
-    rising = transposed(found[1])[:LIVE] * scale_lane
     message = jnp.where(odd, ahead, ahead_t) + pltpu.roll(jnp.where(odd, ahead_t, ahead), LIVE, 1)
-    message = message + pltpu.roll(rising, 2 * LIVE, 1)
     message = jnp.where(lane >= 3 * LIVE, count.astype(F32), message)
     message = jnp.where(lane == 3 * LIVE + 1, scale_row, message)
+    rising = transposed(half[1])[:LIVE] * scale_lane
+    message = message + pltpu.roll(rising, 2 * LIVE, 1)
 
     @pl.when(joined & (g == 0))
     def _():
-        links[chip, core] = message
+        upward[...] = message
         link_up.start()
-        others(GROUP // 2, chip, lambda v: link_copy(v, chip).start())
 
     @pl.when(joined & (g == 1))
     def _():
         piv_up.wait_recv()
         others(GROUP // 2, chip, lambda v: piv_copy(v, chip).start())
+        rest = pltpu.roll(half[0], 2 * LIVE, 1) * pivs[chip, core, 8:9]
         link_up.wait_recv()
+        in_rest = (lane >= 2 * LIVE) & (lane < 3 * LIVE)
+        links[chip, core] = links[chip, core] + jnp.where(in_rest, rest, 0.0)
         others(GROUP // 2, chip, lambda v: link_copy(v, chip).start())
 
-    for k in (0, 2):
-        found[k] = coupling(k)
+    part_copy(0).wait_recv()
+    back = jnp.where(inside[1], part_in[1], 0.0)
+    found[1] = half[1] + transposed(back)[:LIVE]
+
+    @pl.when(joined & (g == 0))
+    def _():
+        links[chip, core] = message + pltpu.roll(back * scale_lane, 2 * LIVE, 1)
+        others(GROUP // 2, chip, lambda v: link_copy(v, chip).start())
+
+    found[2] = coupling(2)
+    part_copy(1).wait_recv()
+    found[0] = half[0] + transposed(jnp.where(inside[0], part_in[0], 0.0))[:LIVE]
     blocks_ref[0] = own
     for k in range(4):
         blocks_ref[k + 1] = pad_rows(found[k], SLOTS)
@@ -378,7 +407,11 @@
 
     for k in range(4):
         halo_copy(k).wait_send()
+    for k in range(2):
         face_copy(k).wait_send()
+        part_copy(k).wait_send()
+        for q in range(8):
+            piece_copy(k + 2, q).wait_send()
 
 
 def assemble(count, modes, kappa, react):
@@ -406,20 +439,27 @@
             pltpu.VMEM((CX, CY, NZ), F32),
             pltpu.VMEM((4, 16, NZ), F32),
             pltpu.VMEM((4, 16, NZ), F32),
+            pltpu.VMEM((2, 2 * LIVE, 4 * NZ), BF16),
             pltpu.VMEM((2, 2 * LIVE, 8 * NZ), BF16),
-            pltpu.VMEM((2, 16, SLOTS, NZ), BF16),
             pltpu.VMEM((2 * LIVE, 8 * NZ), BF16),
             pltpu.VMEM((2 * LIVE, 8 * NZ), BF16),
-            pltpu.VMEM((2, 2 * LIVE, 8 * NZ), BF16),
+            pltpu.VMEM((4, 2 * LIVE, 8 * NZ), BF16),
             pltpu.VMEM((GROUP // 2, 2, LIVE, 128), F32),
             pltpu.VMEM((GROUP // 2, 2, 16, 128), F32),
             pltpu.VMEM((NZ, NZ), BF16),
+            pltpu.VMEM((LIVE, 128), F32),
+            pltpu.VMEM((2, LIVE, 128), F32),
+            pltpu.VMEM((2, LIVE, 128), F32),
             dma((CX,)),
             dma((2,)),
             dma((4,)),
             dma((4,)),
-            dma((4,)),
-            dma((4,)),
+            dma((2,)),
+            dma((2,)),
+            dma((2, 8)),
+            dma((2, 8)),
+            dma((2,)),
+            dma((2,)),
             dma((4,)),
             dma((GROUP // 2,)),
             dma((GROUP // 2,)),

time: 51.7 us -> 52.7 us (1.019)
  Pallas kernels: 50.9 us -> 52 us
    pallas_call x1, Pallas kernels: 29.4 us -> 30.1 us  [assemble(): pl.pallas_call(assemble_kernel, out_shape=(jax.ShapeDtypeStruct((6, SLOTS...]
where the time goes in v1:
time: 52.7 us; the launch traced here: 52.6 us
  Pallas kernels  52 us (99%)
  between operations  0.66 us (1%)
    pallas_call x1, Pallas kernels, assemble(): pl.pallas_call(assemble_kernel, out_shape=(jax.ShapeDtypeStruct((6, SLOTS...  30.1 us
    pallas_call x1, Pallas kernels, factor(): pl.pallas_call(factor_kernel, out_shape=jax.ShapeDtypeStruct((SLOTS, NC),...  21.9 us

profile of v1, /device:TPU:9, one launch (start us, length us, event | category | flops | bytes accessed | tf_op | source)
XLA Modules:
  0.0 52.6 jit_solution(18021950644368873931)
XLA Ops:
  0.7 30.1 %assemble.1 = (f32[6,48,128]{2,1,0:T(8,128)S(1)}, f32[24,40,128]{2,1,0:T(8,128)S(1)}, f32[24,16,128]{2,1,0:T(8,128)S(1)}) custom-call(s32[1]{0:T(128)S(6)} %copy.5.count_ref, bf16[48,16,16,256]{3,2,1,0:T(8,128)(2,1)} %modes_ref.1, bf16[16,16,256]{2,1,0:T(8,128)(2,1)} %kappa_ref.1, bf16[16,16,256]{2,1,0:T(8,128)(2,1)} %react_ref.1), custom_call_target="tpu_custom_call" | custom-call | tf_op jit(solution)/shard_map/assemble/pallas_call | solution.py:421
  30.7 21.9 %factor.1 = f32[48,6144]{1,0:T(8,128)} custom-call(f32[24,40,128]{2,1,0:T(8,128)S(1)} %get-tuple-element.8.links_ref, f32[24,16,128]{2,1,0:T(8,128)S(1)} %get-tuple-element.9.pivots_ref, f32[6,48,128]{2,1,0:T(8,128)S(1)} %get-tuple-element.10.blocks_ref), custom_call_target="tpu_custom_call" | custom-call | tf_op jit(solution)/shard_map/factor/pallas_call | solution.py:743
